TPU v7x, 32 devices: a whole 2x2x4 slice. The times are simulated.
32 devices in a mesh: gx: 8 (over z, core), gy: 4 (over y, x).
Axes of the slice: x: 2, y: 2, z: 4, core: 2. Of those that a mesh axis runs over, the one named last changes fastest.
Arguments:
- pressure0: float32 [4, 128, 512], P(None, 'gx', 'gy'), may hold values from -6 to 6
- saturation0: float32 [4, 128, 512], P(None, 'gx', 'gy'), may hold values from 0.1 to 0.9
- trans_x: float32 [4, 128, 512], P(None, 'gx', 'gy'), may hold values from 0.1 to 2
- trans_y: float32 [4, 128, 512], P(None, 'gx', 'gy'), may hold values from 0.1 to 2
- trans_z: float32 [3, 128, 512], P(None, 'gx', 'gy'), may hold values from 0.05 to 1
- pore_volume: float32 [4, 128, 512], P(None, 'gx', 'gy'), may hold values from 0.5 to 2
- upwind: int32 [4, 128, 512], P(None, 'gx', 'gy'), may hold values from 0 to 63
- well_cell: int32 [8, 4, 64], P('gx', 'gy'), may hold values from 0 to 8191
- well_rate: float32 [8, 4, 64], P('gx', 'gy'), may hold values from -8 to 8
- plan: int32 [2, 8, 4, 64], P(None, 'gx', 'gy'), may hold values from 0 to 2
- observed: float32 [2, 2, 8, 4, 64], P(None, None, 'gx', 'gy'), may hold values from -6 to 6
Outputs:
- grad_x: float32 [4, 128, 512], P(None, 'gx', 'gy')
- grad_y: float32 [4, 128, 512], P(None, 'gx', 'gy')
- grad_z: float32 [3, 128, 512], P(None, 'gx', 'gy')
Inputs may be any that keep to these rules, and one draw needn't show every extreme that they name: `upwind`: bit 3 n + d of an entry is 1 where the cell itself is upstream of its forward face along x, y or layers (d = 0, 1, 2) in step n, 0 where the next cell is. `well_cell`: a cell of the well's own tile, numbered layer by layer, then row, then column. `plan`: 0 shut, 1 half rate, 2 full rate.
All inputs are finite; a program needn't handle non-finite values.
Results may differ from a plain program's by a relative error of at most 0.0001.
Values sent between devices are 32-bit elements; how exact they have to be, the bound alone decides.
No kernel may reach another device: no remote copies, remote signals or barrier semaphores. Data moves between devices by JAX's collectives and lax.ppermute only.
A program may use at most 64 MiB of HBM per device.

v0:
```python
import jax
import jax.numpy as jnp
from jax import lax
from jax.experimental import pallas as pl
from jax.experimental.pallas import tpu as pltpu
from jax.sharding import PartitionSpec as P

time_step = 0.05

GROUPS = {"p": (0, 4), "s": (4, 4), "tx": (8, 4), "ty": (12, 4), "tz": (16, 3), "pv": (19, 4), "up": (23, 4)}
ORDER = ("p", "s", "tx", "ty", "tz", "pv", "up")
COUNT = 27
SLOT = 10
SLOTS = {"p": (0, 10), "tx": (10, 9), "ty": (19, 9), "tz": (28, 9), "pv": (37, 9), "s": (46, 7), "up": (53, 6)}
PACKED = 4
ROWS = 56
HALO = 2 * SLOT
LATE = 99


FIELDS = 11


def pack_rows(*refs):
    p, s, tx, ty, tz, pv, up, cell, rate, plan, observed = refs[:FIELDS]
    own, far, near, upi, cells, rates, plans, seen, sems = refs[FIELDS:]
    targets = [own.at[pl.ds(*GROUPS[name])] for name in ORDER[:6]] + [upi, cells, rates, plans, seen]
    copies = [
        pltpu.make_async_copy(source, target, sems.at[k])
        for k, (source, target) in enumerate(zip(refs[:FIELDS], targets))
    ]
    for copy in copies:
        copy.start()
    for copy in copies:
        copy.wait()
    first = GROUPS["up"][0]
    for layer in range(4):
        own[first + layer] = upi[layer].astype(jnp.float32)
    own[COUNT] = jnp.zeros((16, 128), jnp.float32)
    own[COUNT, 0:1, 0:64] = cells[0].astype(jnp.float32)
    own[COUNT, 1:2, 0:64] = rates[0]
    for n in range(2):
        own[COUNT, 2 + n : 3 + n, 0:64] = plans[n, 0].astype(jnp.float32)
        for k in range(2):
            row = 4 + 2 * n + k
            own[COUNT, row : row + 1, 0:64] = seen[n, k, 0]
    odd = lax.axis_index("gx") & 1
    for g in range(COUNT):
        far[g] = own[g, pl.ds(pl.multiple_of(8 * odd, 8), 8), :]
        near[g] = own[g, pl.ds(pl.multiple_of(8 - 8 * odd, 8), 8), :]
    base = {name: GROUPS[name][0] for name in ORDER}

    blank = jnp.zeros((1, 128), jnp.float32)

    def gathered(*places):
        rows = []
        for layer in (0, 2, 1, 3):
            for name, row in places:
                there = layer < GROUPS[name][1]
                rows.append(own[base[name] + layer, row : row + 1, :] if there else blank)
        return jnp.concatenate([rows[k] for k in (0, 2, 1, 3, 4, 6, 5, 7)], axis=0)

    for_next = [gathered(("p", 7), ("tx", 7))]
    for_next += [jnp.zeros((8, 128), jnp.float32)] * 2
    for_prev = [
        gathered(("p", 8), ("tx", 8)),
        gathered(("ty", 8), ("tz", 8)),
        gathered(("pv", 8), ("p", 9)),
    ]
    for k in range(3):
        far[COUNT + k] = jnp.where(odd == 1, for_next[k], for_prev[k])
        near[COUNT + k] = jnp.where(odd == 1, for_prev[k], for_next[k])
    far[COUNT + 3] = own[COUNT, 0:8, :]
    near[COUNT + 3] = own[COUNT, 0:8, :]


def lanes():
    return lax.broadcasted_iota(jnp.int32, (8, 128), 1)


def in_slot(lane, start, ends, width):
    return ((lane - start - ends * (2 * SLOT - width)) & 63) < width


def sorted_ends(axis, far, near):
    odd = (lax.axis_index(axis) & 1) == 1

    def before(g):
        return jnp.where(odd, near[g], far[g])

    def after(g):
        return jnp.where(odd, far[g], near[g])

    return before, after


def pack_pairs(block, far, near, at):
    odd = lax.axis_index("gy") & 1
    lane = lanes()
    zero = jnp.zeros((8, 128), jnp.float32)
    for pair in range(2):
        ones, twos = {}, {}
        for name in SLOTS:
            first, layers = GROUPS[name]
            ones[name] = block(first + 2 * pair)
            there = 2 * pair + 1 < layers
            twos[name] = pltpu.roll(block(first + 2 * pair + 1), 64, 1) if there else zero
        for out, ends in ((far, odd), (near, 1 - odd)):
            straight = ((lane >> 6) ^ ends) == 0
            part = zero
            for name, (start, width) in SLOTS.items():
                both = jnp.where(straight, ones[name], twos[name])
                both = pltpu.roll(both, start + 2 * SLOT * ends, 1)
                part = jnp.where(in_slot(lane, start, ends, width), both, part)
            out[at + pair] = part


def extra_pair(one, two):
    row = lax.broadcasted_iota(jnp.int32, (8, 128), 0)
    return jnp.where(row < 4, one, pltpu.roll(two, 4, 0)), jnp.where(row < 4, pltpu.roll(one, 4, 0), two)


def pack_own(own, far, near):
    for tile in range(2):
        rows = slice(8 * tile, 8 * tile + 8)
        pack_pairs(lambda g: own[g, rows, :], far, near, 2 * tile)


def pack_cols(own, own_far, own_near, row_far, row_near, far, near):
    low, high = sorted_ends("gx", row_far, row_near)
    for out, part in ((far, own_far), (near, own_near)):
        for at in range(PACKED):
            out[at] = part[at]
    pack_pairs(low, far, near, PACKED)
    pack_pairs(high, far, near, PACKED + 2)
    odd = lax.axis_index("gy") & 1
    lane = lanes()
    both = jnp.where(lane < 64, own[COUNT, 0:8, :], pltpu.roll(low(COUNT + 3), 64, 1))
    extras = extra_pair(low(COUNT), high(COUNT)) + extra_pair(high(COUNT + 1), high(COUNT + 2))
    for out, ends in ((far, odd), (near, 1 - odd)):
        out[2 * PACKED] = both
        part = high(COUNT + 3)
        for k, value in enumerate(extras):
            start = 64 + SLOT * k
            mask = ((lane - start - SLOT * ends) & 127) < SLOT
            part = jnp.where(mask, pltpu.roll(value, start + 2 * SLOT * ends, 1), part)
        out[2 * PACKED + 1] = part


def split3(value):
    hi = value.astype(jnp.bfloat16).astype(jnp.float32)
    rest = value - hi
    mid = rest.astype(jnp.bfloat16).astype(jnp.float32)
    return hi, mid, rest - mid


SRC0, SRC1, OP0, OS0, OP1, OS1, CNT = range(7)


def spread_wells(info, base, to_spot, write):
    width = info.shape[1]
    cell = info[0:1].astype(jnp.int32)
    layer = lax.shift_right_logical(cell, 11)
    place = (lax.shift_right_logical(cell, 7) & 15) + base
    target = jnp.where(place >= 8, layer * 40 + place - 8, -1)
    spot = to_spot(cell & 127)
    hit = lax.broadcasted_iota(jnp.int32, (160, width), 0) == target
    hit = jnp.where(hit, 1.0, 0.0).astype(jnp.bfloat16)
    lane = lax.broadcasted_iota(jnp.int32, (128, width), 0)
    to_lane = jnp.where(lane == spot, 1.0, 0.0).astype(jnp.bfloat16)
    rate = info[1:2] * 0.5
    values = [rate * info[2:3], rate * info[3:4]] + [info[k : k + 1] for k in range(4, 8)]
    for number, value in enumerate(values):
        total = None
        for part in split3(value):
            part = jnp.broadcast_to(part, (16, width)).astype(jnp.bfloat16)
            left = hit * jnp.concatenate([part] * 10, axis=0)
            term = dot(left, to_lane)
            total = term if total is None else total + term
        write(number, total)
    write(CNT, dot(hit, to_lane))


def dot(left, right):
    return lax.dot_general(left, right, (((1,), (1,)), ((), ())), preferred_element_type=jnp.float32)


def list_block(info):
    return lax.shift_right_logical(lax.broadcasted_iota(jnp.int32, (1, info.shape[1]), 1), 6)


SCRATCH = (4,) * 11 + (11,) * 4 + (4,) * 9


def simulate(fld, dense, upi, scratch, emit_x, emit_y, emit_z, tile_done=None):
    (rcp, tym, q0, p1, q1, p2, f0, d0, s1, f1, d1, fup0, fup1, dp1, dp2,
     sig2, psi2, psi1, mup2, muq1, mup1, muq0, flux, rest) = scratch
    PB, SB, XB, YB, ZB, VB = (GROUPS[name][0] for name in ORDER[:6])

    def here(ref, k, t):
        return ref[k, 8 * t : 8 * t + 8, :]

    def down(ref, k, t):
        return ref[k, 8 * t + 1 : 8 * t + 9, :]

    def above(ref, k, t):
        return ref[k, 8 * t - 1 : 8 * t + 7, :]

    def put(ref, k, t, value):
        ref[k, 8 * t : 8 * t + 8, :] = value

    def right(value):
        return pltpu.roll(value, 127, 1)

    def left(value):
        return pltpu.roll(value, 1, 1)

    for k in range(4):
        for t in range(1, 6):
            beyond = right(here(fld, VB + k, t))
            put(fld, YB + k, t, jnp.where(beyond == 0.0, 0.0, here(fld, YB + k, t)))
        last = slice(31, 32)
        fld[XB + k, last, :] = jnp.where(fld[VB + k, 32:33, :] == 0.0, 0.0, fld[XB + k, last, :])
    for t in range(1, 6):
        for k in range(4):
            volume = here(fld, VB + k, t)
            volume = jnp.where(volume == 0.0, 1.0, volume)
            put(fld, VB + k, t, volume)
            west = left(here(fld, YB + k, t))
            put(tym, k, t, west)
            total = volume + (here(fld, XB + k, t) + above(fld, XB + k, t)) + (here(fld, YB + k, t) + west)
            if k < 3:
                total = total + here(fld, ZB + k, t)
            if k > 0:
                total = total + here(fld, ZB + k - 1, t)
            put(rcp, k, t, 1.0 / total)

    def neighbours(ref, base, k, t):
        value = here(ref, base + k, t)
        total = here(fld, XB + k, t) * down(ref, base + k, t) + above(fld, XB + k, t) * above(ref, base + k, t)
        total = total + (here(fld, YB + k, t) * right(value) + here(tym, k, t) * left(value))
        if k < 3:
            total = total + here(fld, ZB + k, t) * here(ref, base + k + 1, t)
        if k > 0:
            total = total + here(fld, ZB + k - 1, t) * here(ref, base + k - 1, t)
        return total

    def relax(out, ref, base, old, old_base, source, tiles):
        for t in tiles:
            for k in range(4):
                total = here(fld, VB + k, t) * here(old, old_base + k, t) + here(dense.at[source], k, t)
                put(out, k, t, (total + neighbours(ref, base, k, t)) * here(rcp, k, t))

    def put_mobility(value, k, t, mobile, slope):
        rest_of = 1.0 - value
        wetted = value * value
        inverse = 1.0 / (wetted + 0.5 * rest_of * rest_of)
        put(mobile, k, t, wetted * inverse)
        put(slope, k, t, value * rest_of * (inverse * inverse))

    def bit(k, t, number):
        return (here(upi, k, t) & (1 << number)) != 0

    def transport(pressure, sat, sat_base, mobile, n, fup, dp, finish):
        for t in range(1, 5):
            below = None
            for k in range(4):
                mob = here(mobile, k, t)
                pres = here(pressure, k, t)
                drop_x = pres - down(pressure, k, t)
                drop_y = pres - right(pres)
                up_x = jnp.where(bit(k, t, 3 * n), mob, down(mobile, k, t))
                up_y = jnp.where(bit(k, t, 3 * n + 1), mob, right(mob))
                put(fup, k, t, up_x)
                put(fup, 4 + k, t, up_y)
                put(dp, k, t, drop_x)
                put(dp, 4 + k, t, drop_y)
                flux_x = here(fld, XB + k, t) * up_x * drop_x
                flux_y = here(fld, YB + k, t) * up_y * drop_y
                put(flux, k, t, flux_x)
                net = (flux_x - above(flux, k, t)) + (flux_y - left(flux_y))
                if k > 0:
                    net = net - below
                if k < 3:
                    drop_z = pres - here(pressure, k + 1, t)
                    up_z = jnp.where(bit(k, t, 3 * n + 2), mob, here(mobile, k + 1, t))
                    put(fup, 8 + k, t, up_z)
                    put(dp, 8 + k, t, drop_z)
                    below = here(fld, ZB + k, t) * up_z * drop_z
                    net = net + below
                finish(here(sat, sat_base + k, t) - time_step * net / here(fld, VB + k, t), k, t)

    tiles = range(1, 5)
    relax(q0, fld, PB, fld, PB, SRC0, range(1, 6))
    relax(p1, q0, 0, fld, PB, SRC0, tiles)
    for t in tiles:
        for k in range(4):
            put_mobility(here(fld, SB + k, t), k, t, f0, d0)

    def finish_first(moved, k, t):
        put(s1, k, t, moved)
        put_mobility(moved, k, t, f1, d1)

    transport(p1, fld, SB, f0, 0, fup0, dp1, finish_first)
    relax(q1, p1, 0, p1, 0, SRC1, tiles)
    relax(p2, q1, 0, p1, 0, SRC1, tiles)

    def finish_second(moved, k, t):
        miss = here(dense.at[CNT], k, t) * moved - here(dense.at[OS1], k, t)
        put(sig2, k, t, miss)
        put(psi2, k, t, time_step * miss / here(fld, VB + k, t))

    transport(p2, s1, 0, f1, 1, fup1, dp2, finish_second)

    for t in tiles:
        below_h = below_r = None
        for k in range(4):
            psi = here(psi2, k, t)
            phi_x = (down(psi2, k, t) - psi) * here(fld, XB + k, t)
            phi_y = (right(psi) - psi) * here(fld, YB + k, t)
            h_x = phi_x * here(fup1, k, t)
            h_y = phi_y * here(fup1, 4 + k, t)
            k_x = phi_x * here(dp2, k, t)
            k_y = phi_y * here(dp2, 4 + k, t)
            s_x = jnp.where(bit(k, t, 3), k_x, 0.0)
            s_y = jnp.where(bit(k, t, 4), k_y, 0.0)
            put(flux, k, t, h_x)
            put(rest, k, t, k_x - s_x)
            press = (h_x - above(flux, k, t)) + (h_y - left(h_y))
            satur = (s_x + above(rest, k, t)) + (s_y + left(k_y - s_y))
            if k > 0:
                press = press - below_h
                satur = satur + below_r
            if k < 3:
                phi_z = (here(psi2, k + 1, t) - psi) * here(fld, ZB + k, t)
                below_h = phi_z * here(fup1, 8 + k, t)
                k_z = phi_z * here(dp2, 8 + k, t)
                s_z = jnp.where(bit(k, t, 5), k_z, 0.0)
                below_r = k_z - s_z
                press = press + below_h
                satur = satur + s_z
            count = here(dense.at[CNT], k, t)
            press = press + (count * here(p2, k, t) - here(dense.at[OP1], k, t))
            put(mup2, k, t, press * here(rcp, k, t))
            sigma = here(sig2, k, t) + satur * here(d1, k, t)
            sigma = sigma + (count * here(s1, k, t) - here(dense.at[OS0], k, t))
            put(psi1, k, t, time_step * sigma / here(fld, VB + k, t))

    for t in tiles:
        for k in range(4):
            put(muq1, k, t, neighbours(mup2, 0, k, t) * here(rcp, k, t))

    for t in tiles:
        below_h = None
        for k in range(4):
            psi = here(psi1, k, t)
            h_x = (down(psi1, k, t) - psi) * here(fld, XB + k, t) * here(fup0, k, t)
            h_y = (right(psi) - psi) * here(fld, YB + k, t) * here(fup0, 4 + k, t)
            put(flux, k, t, h_x)
            press = (h_x - above(flux, k, t)) + (h_y - left(h_y))
            if k > 0:
                press = press - below_h
            if k < 3:
                below_h = (here(psi1, k + 1, t) - psi) * here(fld, ZB + k, t) * here(fup0, 8 + k, t)
                press = press + below_h
            count = here(dense.at[CNT], k, t)
            press = press + (count * here(p1, k, t) - here(dense.at[OP0], k, t))
            press = press + here(fld, VB + k, t) * (here(mup2, k, t) + here(muq1, k, t))
            press = press + neighbours(muq1, 0, k, t)
            put(mup1, k, t, press * here(rcp, k, t))

    for t in range(2, 5):
        for k in range(4):
            put(muq0, k, t, neighbours(mup1, 0, k, t) * here(rcp, k, t))

    stages = (
        (mup2, q1, 0, p2, 0),
        (muq1, p1, 0, q1, 0),
        (mup1, q0, 0, p1, 0),
        (muq0, fld, PB, q0, 0),
    )
    for t in range(2, 4):
        for k in range(4):
            sum_x = sum_y = sum_z = 0.0
            for psi, fup, dp in ((psi2, fup1, dp2), (psi1, fup0, dp1)):
                mid = here(psi, k, t)
                sum_x = sum_x + (down(psi, k, t) - mid) * here(fup, k, t) * here(dp, k, t)
                sum_y = sum_y + (right(mid) - mid) * here(fup, 4 + k, t) * here(dp, 4 + k, t)
                if k < 3:
                    sum_z = sum_z + (here(psi, k + 1, t) - mid) * here(fup, 8 + k, t) * here(dp, 8 + k, t)
            for mu, value, base, out, out_base in stages:
                mu_c, v_c, o_c = here(mu, k, t), here(value, base + k, t), here(out, out_base + k, t)
                mu_d, v_d, o_d = down(mu, k, t), down(value, base + k, t), down(out, out_base + k, t)
                sum_x = sum_x + (mu_c * (v_d - o_c) + mu_d * (v_c - o_d))
                sum_y = sum_y + (mu_c * (right(v_c) - o_c) + right(mu_c) * (v_c - right(o_c)))
                if k < 3:
                    mu_u = here(mu, k + 1, t)
                    v_u = here(value, base + k + 1, t)
                    o_u = here(out, out_base + k + 1, t)
                    sum_z = sum_z + (mu_c * (v_u - o_c) + mu_u * (v_c - o_u))
            emit_x(k, t, jnp.where(here(fld, XB + k, t) == 0.0, 0.0, sum_x))
            emit_y(k, t, jnp.where(here(fld, YB + k, t) == 0.0, 0.0, sum_y))
            if k < 3:
                emit_z(k, t, sum_z)
        if tile_done is not None:
            tile_done(t)


PLACES = (
    (("p", 7), ("tx", 7)),
    (("p", 40), ("tx", 40)),
    (("ty", 40), ("tz", 40)),
    (("pv", 40), ("p", 41)),
)


def put_beyond(fld, value, places):
    for block, (name, row) in enumerate(places):
        first, layers = GROUPS[name]
        for layer in range(layers):
            k = 4 * (layer & 1) + 2 * block + layer // 2
            fld[first + layer, row : row + 1, :] = value[k : k + 1]


def model_center(own, row_far, row_near, grads, edge, edge_dense, fld, dense, upi, *scratch):
    low, high = sorted_ends("gx", row_far, row_near)
    lane = lanes()

    early = lane < LATE

    def edge_of(value):
        return jnp.where(early, pltpu.roll(value, HALO, 1), value)

    for g in range(COUNT):
        for k, block in enumerate((low(g), own[g, 0:8, :], own[g, 8:16, :], high(g))):
            rows = slice(8 + 8 * k, 16 + 8 * k)
            fld[g, rows, :] = block
            edge[g, rows, :] = edge_of(block)
            if g >= GROUPS["up"][0]:
                upi[g - GROUPS["up"][0], rows, :] = block.astype(jnp.int32)
    for value, places in zip([low(COUNT)] + [high(COUNT + k) for k in range(3)], PLACES):
        for out, rows in ((fld, value), (edge, edge_of(value))):
            put_beyond(out, rows, places)

    info = jnp.concatenate(
        [own[COUNT, 0:8, 0:64], low(COUNT + 3)[:, 0:64], high(COUNT + 3)[:, 0:64]], axis=1
    )
    block = list_block(info)
    base = jnp.where(block == 0, 16, jnp.where(block == 1, 0, 32))

    def write_center(number, total):
        for k in range(4):
            dense[number, k, 8:48, :] = total[40 * k : 40 * k + 40]

    def write_edge(number, total):
        for k in range(4):
            edge_dense[number, k, 8:48, :] = total[40 * k : 40 * k + 40]

    def edge_lane(col):
        return jnp.where(col < LATE - HALO, col + HALO, jnp.where(col >= LATE, col, -1))

    spread_wells(info, base, lambda col: col, write_center)
    spread_wells(info, base, edge_lane, write_edge)

    def emit(first):
        def write(k, t, value):
            grads[first + k, 8 * t - 16 : 8 * t - 8, :] = value

        return write

    simulate(fld, dense, upi, scratch, emit(0), emit(4), emit(8))


def model_edge(
    col_far, col_near, edge, edge_dense, center, grad_x, grad_y, grad_z, first_rows, last_rows, sems, fld, dense, upi,
    *scratch
):
    before, after = sorted_ends("gy", col_far, col_near)
    odd = lax.axis_index("gy") & 1
    lane = lanes()
    beside = lane < HALO
    for name, (start, width) in SLOTS.items():
        far_cols = in_slot(lane, start, 1 - odd, width)
        first, layers = GROUPS[name]
        for layer in range(layers):
            for k, at in enumerate((PACKED, 0, 2, PACKED + 2)):
                rows = slice(8 + 8 * k, 16 + 8 * k)
                both = jnp.where(far_cols, col_far[at + layer // 2], col_near[at + layer // 2])
                both = pltpu.roll(both, (64 * (layer & 1) - start) % 128, 1)
                block = jnp.where(beside, both, edge[first + layer, rows, :])
                if name == "up":
                    upi[layer, rows, :] = block.astype(jnp.int32)
                else:
                    fld[first + layer, rows, :] = block
    for number, places in enumerate(PLACES):
        for half in range(2):
            start = 64 + SLOT * (2 * (number // 2) + half)
            mask = ((lane - start - SLOT * (1 - odd)) & 127) < SLOT
            both = jnp.where(mask, col_far[2 * PACKED + 1], col_near[2 * PACKED + 1])
            value = pltpu.roll(both, 128 - start, 1)
            for block, (name, row) in enumerate(places):
                for pair in range(2):
                    layer = 2 * pair + half
                    if layer < GROUPS[name][1]:
                        k = 4 * (number & 1) + 2 * block + pair
                        at = (GROUPS[name][0] + layer, slice(row, row + 1), slice(None))
                        fld[at] = jnp.where(beside[0:1], value[k : k + 1], edge[at])
    first, second = 2 * PACKED, 2 * PACKED + 1
    own_lists = [before(first)[:, 0:64], after(first)[:, 0:64]]
    low_lists = [before(first)[:, 64:128], after(first)[:, 64:128]]
    high_lists = [before(second)[:, 0:64], after(second)[:, 0:64]]
    info = jnp.concatenate(own_lists + low_lists + high_lists, axis=1)
    block = list_block(info)
    base = jnp.where(block < 2, 16, jnp.where(block < 4, 0, 32))
    ahead = (block & 1) == 1

    def beside_lane(col):
        last = jnp.where(col >= 128 - SLOT, col - 128 + 2 * SLOT, -1)
        return jnp.where(ahead, jnp.where(col < SLOT, col, -1), last)

    def write_beside(number, total):
        for k in range(4):
            dense[number, k, 8:48, :] = total[40 * k : 40 * k + 40] + edge_dense[number, k, 8:48, :]

    spread_wells(info, base, beside_lane, write_beside)

    def emit(group):
        def write(k, t, value):
            rows = slice(8 * t - 16, 8 * t - 8)
            value = jnp.where(lane < 64, pltpu.roll(value, 128 - HALO, 1), value)
            inner = (lane >= SLOT - 1) & (lane < 128 - SLOT)
            (first_rows, last_rows)[t - 2][group + k] = jnp.where(inner, center[group + k, rows, :], value)

        return write

    def send(t):
        copies = []
        for k, (out, group) in enumerate(((grad_x, 0), (grad_y, 4), (grad_z, 8))):
            source = (first_rows, last_rows)[t - 2].at[pl.ds(group, out.shape[0])]
            target = out.at[:, pl.ds(8 * t - 16, 8), :]
            copies.append(pltpu.make_async_copy(source, target, sems.at[3 * (t - 2) + k]))
            copies[-1].start()
        return copies

    copies = []
    simulate(fld, dense, upi, scratch, emit(0), emit(4), emit(8), lambda t: copies.extend(send(t)))
    for copy in copies:
        copy.wait()


def swapped(value, axis, first):
    count = lax.axis_size(axis)
    pairs = []
    for i in range(first, count - 1, 2):
        pairs += [(i, i + 1), (i + 1, i)]
    return lax.ppermute(value, axis, pairs)


def on_device(p, s, tx, ty, tz, pv, up, cell, rate, plan, observed):
    f32 = jnp.float32

    def shape(*dims):
        return jax.ShapeDtypeStruct(dims, f32)

    limit = pltpu.CompilerParams(vmem_limit_bytes=24 * 1024 * 1024)
    inputs = (p, s, tx, ty, tz, pv, up, cell, rate, plan, observed)
    inputs = [pltpu.with_memory_space_constraint(value, pltpu.HBM) for value in inputs]
    strip = shape(COUNT + 4, 8, 128)
    own, far, near = pl.pallas_call(
        pack_rows,
        out_shape=(shape(COUNT + 1, 16, 128), strip, strip),
        in_specs=[pl.BlockSpec(memory_space=pltpu.HBM)] * len(inputs),
        scratch_shapes=[pltpu.VMEM(value.shape, value.dtype) for value in inputs[6:]]
        + [pltpu.SemaphoreType.DMA((len(inputs),))],
        compiler_params=limit,
        name="pack_rows",
    )(*inputs)
    row_far = swapped(far, "gx", 1)
    row_near = swapped(near, "gx", 0)
    hide = pl.CostEstimate(flops=10**11, bytes_accessed=1 << 28, transcendentals=0)
    strip = shape(PACKED, 8, 128)
    own_far, own_near = pl.pallas_call(
        pack_own,
        out_shape=(strip, strip),
        compiler_params=limit,
        cost_estimate=hide,
        name="pack_own",
    )(own)
    strip = shape(2 * PACKED + 2, 8, 128)
    far, near = pl.pallas_call(
        pack_cols,
        out_shape=(strip, strip),
        compiler_params=limit,
        name="pack_cols",
    )(own, own_far, own_near, row_far, row_near)
    col_far = swapped(far, "gy", 1)
    col_near = swapped(near, "gy", 0)
    scratch = [pltpu.VMEM((COUNT, ROWS, 128), f32), pltpu.VMEM((7, 4, ROWS, 128), f32)]
    scratch += [pltpu.VMEM((4, ROWS, 128), jnp.int32)]
    scratch += [pltpu.VMEM((count, ROWS, 128), f32) for count in SCRATCH]
    center, edge, edge_dense = pl.pallas_call(
        model_center,
        out_shape=(shape(11, 16, 128), shape(COUNT, ROWS, 128), shape(7, 4, ROWS, 128)),
        scratch_shapes=scratch,
        compiler_params=limit,
        cost_estimate=hide,
        name="model_center",
    )(own, row_far, row_near)
    return pl.pallas_call(
        model_edge,
        out_shape=(shape(*tx.shape), shape(*ty.shape), shape(*tz.shape)),
        out_specs=(pl.BlockSpec(memory_space=pltpu.HBM),) * 3,
        scratch_shapes=[pltpu.VMEM((11, 8, 128), f32)] * 2 + [pltpu.SemaphoreType.DMA((6,))] + scratch,
        compiler_params=limit,
        name="model_edge",
    )(col_far, col_near, edge, edge_dense, center)


def solution(mesh):
    cells = P(None, "gx", "gy")
    in_specs = (cells,) * 7 + (
        P("gx", "gy", None),
        P("gx", "gy", None),
        P(None, "gx", "gy", None),
        P(None, None, "gx", "gy", None),
    )
    return jax.shard_map(
        on_device, mesh=mesh, in_specs=in_specs, out_specs=(cells,) * 3, check_vma=False
    )
```

profile of v0, /device:TPU:0, one launch (start us, length us, event | category | flops | bytes accessed | tf_op | source)
XLA Modules:
  0.0 18.0 jit_solution(5009439726892786275)
XLA Ops:
  0.6 1.0 %pack_rows.1 = (f32[28,16,128]{2,1,0:T(8,128)S(1)}, f32[31,8,128]{2,1,0:T(8,128)S(1)}, f32[31,8,128]{2,1,0:T(8,128)S(1)}) custom-call(f32[4,16,128]{2,1,0:T(8,128)} %refs_0_.1, f32[4,16,128]{2,1,0:T(8,128)} %refs_1_.1, f32[4,16,128]{2,1,0:T(8,128)} %refs_2_.1, f32[4,16,128]{2,1,0:T(8,128)} %refs_3_.1, f32[3,16,128]{2,1,0:T(8,128)} %refs_4_.1, ...), custom_call_target="tpu_custom_call" | custom-call | tf_op jit(solution)/shard_map/pack_rows/pallas_call | solution.py:569
  1.6 0.7 %collective-permute-start = (f32[31,8,128]{2,1,0:T(8,128)S(1)}, f32[31,8,128]{2,1,0:T(8,128)S(1)}, u32[]{:S(2)}, u32[]{:S(2)}) collective-permute-start(f32[31,8,128]{2,1,0:T(8,128)S(1)} %get-tuple-element.16), channel_id=1, source_target_pairs={{4,8},{8,4},{12,16},{16,12},{20,24},{24,20},{5,9},{9,5},{13,17},{1... | collective-permute-start | bytes 380936 | tf_op jit(solution)/shard_map/ppermute | solution.py:556
  2.3 4.4 %collective-permute-start.1 = (f32[31,8,128]{2,1,0:T(8,128)S(1)}, f32[31,8,128]{2,1,0:T(8,128)S(1)}, u32[]{:S(2)}, u32[]{:S(2)}) collective-permute-start(f32[31,8,128]{2,1,0:T(8,128)S(1)} %get-tuple-element.17), channel_id=1, source_target_pairs={{0,4},{4,0},{8,12},{12,8},{16,20},{20,16},{24,28},{28,24},{1,5},{5... | collective-permute-start | bytes 380936 | tf_op jit(solution)/shard_map/ppermute | solution.py:556
  6.8 0.2 %pack_own.1 = (f32[4,8,128]{2,1,0:T(8,128)S(1)}, f32[4,8,128]{2,1,0:T(8,128)S(1)}) custom-call(f32[28,16,128]{2,1,0:T(8,128)S(1)} %get-tuple-element.13.own), custom_call_target="tpu_custom_call" | custom-call | flops 99999997952 | bytes 268435456 | tf_op jit(solution)/shard_map/pack_own/pallas_call | solution.py:582
  7.0 0.0 collective-permute-done.row_far
  7.0 0.8 %collective-permute-done.1.row_near = f32[31,8,128]{2,1,0:T(8,128)S(1)} collective-permute-done((f32[31,8,128]{2,1,0:T(8,128)S(1)}, f32[31,8,128]{2,1,0:T(8,128)S(1)}, u32[]{:S(2)}, u32[]{:S(2)}) %collective-permute-start.1) | collective-permute-done | bytes 127008 | tf_op jit(solution)/shard_map/ppermute | solution.py:556
  7.7 0.2 %pack_cols.1 = (f32[10,8,128]{2,1,0:T(8,128)S(1)}, f32[10,8,128]{2,1,0:T(8,128)S(1)}) custom-call(f32[28,16,128]{2,1,0:T(8,128)S(1)} %get-tuple-element.13.own, f32[4,8,128]{2,1,0:T(8,128)S(1)} %get-tuple-element.14.own_far, f32[4,8,128]{2,1,0:T(8,128)S(1)} %get-tuple-element.15.own_near, f32[31,8,128]{2,1,0:T(8,128)S(1)} %collective-permute-done.row_far, ...), custom_call_target="tpu_custom_call" | custom-call | tf_op jit(solution)/shard_map/pack_cols/pallas_call | solution.py:590
  7.9 0.7 %collective-permute-start.2 = (f32[10,8,128]{2,1,0:T(8,128)S(1)}, f32[10,8,128]{2,1,0:T(8,128)S(1)}, u32[]{:S(2)}, u32[]{:S(2)}) collective-permute-start(f32[10,8,128]{2,1,0:T(8,128)S(1)} %get-tuple-element.18), channel_id=1, source_target_pairs={{1,2},{2,1},{5,6},{6,5},{9,10},{10,9},{13,14},{14,13},{17,18},{18,... | collective-permute-start | bytes 122888 | tf_op jit(solution)/shard_map/ppermute | solution.py:556
  8.6 4.3 %collective-permute-start.3 = (f32[10,8,128]{2,1,0:T(8,128)S(1)}, f32[10,8,128]{2,1,0:T(8,128)S(1)}, u32[]{:S(2)}, u32[]{:S(2)}) collective-permute-start(f32[10,8,128]{2,1,0:T(8,128)S(1)} %get-tuple-element.19), channel_id=1, source_target_pairs={{0,1},{1,0},{2,3},{3,2},{4,5},{5,4},{6,7},{7,6},{8,9},{9,8},{10,11... | collective-permute-start | bytes 122888 | tf_op jit(solution)/shard_map/ppermute | solution.py:556
  12.9 1.5 %model_center.1 = (f32[11,16,128]{2,1,0:T(8,128)S(1)}, f32[27,56,128]{2,1,0:T(8,128)S(1)}, f32[7,4,56,128]{3,2,1,0:T(8,128)S(1)}) custom-call(f32[28,16,128]{2,1,0:T(8,128)S(1)} %get-tuple-element.13.own, f32[31,8,128]{2,1,0:T(8,128)S(1)} %collective-permute-done.row_far, f32[31,8,128]{2,1,0:T(8,128)S(1)} %collective-permute-done.1.row_near), custom_call_target="tpu_custom_call" | custom-call | flops 99999997952 | bytes 268435456 | tf_op jit(solution)/shard_map/model_center/pallas_call | solution.py:601
  14.4 0.0 collective-permute-done.2.col_far
  14.4 1.2 %collective-permute-done.3.col_near = f32[10,8,128]{2,1,0:T(8,128)S(1)} collective-permute-done((f32[10,8,128]{2,1,0:T(8,128)S(1)}, f32[10,8,128]{2,1,0:T(8,128)S(1)}, u32[]{:S(2)}, u32[]{:S(2)}) %collective-permute-start.3) | collective-permute-done | bytes 40992 | tf_op jit(solution)/shard_map/ppermute | solution.py:556
  15.6 2.4 %model_edge.1 = (f32[4,16,128]{2,1,0:T(8,128)}, f32[4,16,128]{2,1,0:T(8,128)}, f32[3,16,128]{2,1,0:T(8,128)}) custom-call(f32[10,8,128]{2,1,0:T(8,128)S(1)} %collective-permute-done.2.col_far, f32[10,8,128]{2,1,0:T(8,128)S(1)} %collective-permute-done.3.col_near, f32[27,56,128]{2,1,0:T(8,128)S(1)} %get-tuple-element.20.edge, ...), custom_call_target="tpu_custom_call" | custom-call | tf_op jit(solution)/shard_map/model_edge/pallas_call | solution.py:609
Async XLA Ops:
  1.6 5.3 %collective-permute-start = (f32[31,8,128]{2,1,0:T(8,128)S(1)}, f32[31,8,128]{2,1,0:T(8,128)S(1)}, u32[]{:S(2)}, u32[]{:S(2)}) collective-permute-start(f32[31,8,128]{2,1,0:T(8,128)S(1)} %get-tuple-element.16), channel_id=1, source_target_pairs={{4,8},{8,4},{12,16},{16,12},{20,24},{24,20},{5,9},{9,5},{13,17},{1... | collective-permute-start | bytes 380936 | tf_op jit(solution)/shard_map/ppermute | solution.py:556
  2.3 5.4 %collective-permute-start.1 = (f32[31,8,128]{2,1,0:T(8,128)S(1)}, f32[31,8,128]{2,1,0:T(8,128)S(1)}, u32[]{:S(2)}, u32[]{:S(2)}) collective-permute-start(f32[31,8,128]{2,1,0:T(8,128)S(1)} %get-tuple-element.17), channel_id=1, source_target_pairs={{0,4},{4,0},{8,12},{12,8},{16,20},{20,16},{24,28},{28,24},{1,5},{5... | collective-permute-start | bytes 380936 | tf_op jit(solution)/shard_map/ppermute | solution.py:556
  7.9 6.5 %collective-permute-start.2 = (f32[10,8,128]{2,1,0:T(8,128)S(1)}, f32[10,8,128]{2,1,0:T(8,128)S(1)}, u32[]{:S(2)}, u32[]{:S(2)}) collective-permute-start(f32[10,8,128]{2,1,0:T(8,128)S(1)} %get-tuple-element.18), channel_id=1, source_target_pairs={{1,2},{2,1},{5,6},{6,5},{9,10},{10,9},{13,14},{14,13},{17,18},{18,... | collective-permute-start | bytes 122888 | tf_op jit(solution)/shard_map/ppermute | solution.py:556
  8.6 7.0 %collective-permute-start.3 = (f32[10,8,128]{2,1,0:T(8,128)S(1)}, f32[10,8,128]{2,1,0:T(8,128)S(1)}, u32[]{:S(2)}, u32[]{:S(2)}) collective-permute-start(f32[10,8,128]{2,1,0:T(8,128)S(1)} %get-tuple-element.19), channel_id=1, source_target_pairs={{0,1},{1,0},{2,3},{3,2},{4,5},{5,4},{6,7},{7,6},{8,9},{9,8},{10,11... | collective-permute-start | bytes 122888 | tf_op jit(solution)/shard_map/ppermute | solution.py:556
where the time goes:
time: 18.2 us; the launch traced here: 18 us
  starting transfers between devices  10.1 us (55%)
  Pallas kernels  5.29 us (29%)
  waiting for transfers between devices  1.96 us (11%)
  between operations  0.68 us (4%)
    ppermute x4, starting transfers between devices, swapped(): return lax.ppermute(value, axis, pairs)  10.1 us
    pallas_call x1, Pallas kernels, on_device(): pl.pallas_call(model_edge, out_shape=(shape(*tx.shape), shape(*ty.shape),...  2.41 us
    ppermute x4, waiting for transfers between devices, swapped(): return lax.ppermute(value, axis, pairs)  1.96 us
    pallas_call x1, Pallas kernels, on_device(): pl.pallas_call(model_center, out_shape=(shape(11, 16, 128), shape(COUNT,...  1.5 us
    pallas_call x1, Pallas kernels, on_device(): pl.pallas_call(pack_rows, out_shape=(shape(COUNT + 1, 16, 128), strip, st...  0.99 us
  transfers between devices with their start and end apart: 4, of which 2 were waited for; matrix products, arithmetic and copies ran while one was open for 0% of the time, Pallas kernels for 9%

commit v1 on v0

--- a/solution.py
+++ b/solution.py
@@ -31,11 +31,18 @@
     ]
     for copy in copies:
         copy.start()
-    for copy in copies:
+    odd = lax.axis_index("gx") & 1
+    for name, copy in zip(ORDER, copies):
         copy.wait()
-    first = GROUPS["up"][0]
-    for layer in range(4):
-        own[first + layer] = upi[layer].astype(jnp.float32)
+        first, layers = GROUPS[name]
+        for layer in range(layers):
+            g = first + layer
+            if name == "up":
+                own[g] = upi[layer].astype(jnp.float32)
+            far[g] = own[g, pl.ds(pl.multiple_of(8 * odd, 8), 8), :]
+            near[g] = own[g, pl.ds(pl.multiple_of(8 - 8 * odd, 8), 8), :]
+    for copy in copies[len(ORDER) :]:
+        copy.wait()
     own[COUNT] = jnp.zeros((16, 128), jnp.float32)
     own[COUNT, 0:1, 0:64] = cells[0].astype(jnp.float32)
     own[COUNT, 1:2, 0:64] = rates[0]
@@ -44,10 +51,6 @@
         for k in range(2):
             row = 4 + 2 * n + k
             own[COUNT, row : row + 1, 0:64] = seen[n, k, 0]
-    odd = lax.axis_index("gx") & 1
-    for g in range(COUNT):
-        far[g] = own[g, pl.ds(pl.multiple_of(8 * odd, 8), 8), :]
-        near[g] = own[g, pl.ds(pl.multiple_of(8 - 8 * odd, 8), 8), :]
     base = {name: GROUPS[name][0] for name in ORDER}
 
     blank = jnp.zeros((1, 128), jnp.float32)
@@ -126,7 +129,7 @@
         pack_pairs(lambda g: own[g, rows, :], far, near, 2 * tile)
 
 
-def pack_cols(own, own_far, own_near, row_far, row_near, far, near):
+def pack_cols(own, own_far, own_near, row_far, row_near, near, far):
     low, high = sorted_ends("gx", row_far, row_near)
     for out, part in ((far, own_far), (near, own_near)):
         for at in range(PACKED):
@@ -157,14 +160,14 @@
 SRC0, SRC1, OP0, OS0, OP1, OS1, CNT = range(7)
 
 
-def spread_wells(info, base, to_spot, write):
+def spread_wells(info, base, rows_of, count, to_spot, write):
     width = info.shape[1]
     cell = info[0:1].astype(jnp.int32)
     layer = lax.shift_right_logical(cell, 11)
     place = (lax.shift_right_logical(cell, 7) & 15) + base
-    target = jnp.where(place >= 8, layer * 40 + place - 8, -1)
-    spot = to_spot(cell & 127)
-    hit = lax.broadcasted_iota(jnp.int32, (160, width), 0) == target
+    target = jnp.where(place >= 8, rows_of(layer) + place - 8, -1)
+    spot = to_spot(layer, cell & 127)
+    hit = lax.broadcasted_iota(jnp.int32, (count, width), 0) == target
     hit = jnp.where(hit, 1.0, 0.0).astype(jnp.bfloat16)
     lane = lax.broadcasted_iota(jnp.int32, (128, width), 0)
     to_lane = jnp.where(lane == spot, 1.0, 0.0).astype(jnp.bfloat16)
@@ -174,7 +177,7 @@
         total = None
         for part in split3(value):
             part = jnp.broadcast_to(part, (16, width)).astype(jnp.bfloat16)
-            left = hit * jnp.concatenate([part] * 10, axis=0)
+            left = hit * jnp.concatenate([part] * (count // 16), axis=0)
             term = dot(left, to_lane)
             total = term if total is None else total + term
         write(number, total)
@@ -456,11 +459,11 @@
         for k in range(4):
             edge_dense[number, k, 8:48, :] = total[40 * k : 40 * k + 40]
 
-    def edge_lane(col):
+    def edge_lane(layer, col):
         return jnp.where(col < LATE - HALO, col + HALO, jnp.where(col >= LATE, col, -1))
 
-    spread_wells(info, base, lambda col: col, write_center)
-    spread_wells(info, base, edge_lane, write_edge)
+    spread_wells(info, base, lambda layer: layer * 40, 160, lambda layer, col: col, write_center)
+    spread_wells(info, base, lambda layer: layer * 40, 160, edge_lane, write_edge)
 
     def emit(first):
         def write(k, t, value):
@@ -472,7 +475,7 @@
 
 
 def model_edge(
-    col_far, col_near, edge, edge_dense, center, grad_x, grad_y, grad_z, first_rows, last_rows, sems, fld, dense, upi,
+    col_near, col_far, edge, edge_dense, center, grad_x, grad_y, grad_z, first_rows, last_rows, sems, fld, dense, upi,
     *scratch
 ):
     before, after = sorted_ends("gy", col_far, col_near)
@@ -514,15 +517,19 @@
     base = jnp.where(block < 2, 16, jnp.where(block < 4, 0, 32))
     ahead = (block & 1) == 1
 
-    def beside_lane(col):
-        last = jnp.where(col >= 128 - SLOT, col - 128 + 2 * SLOT, -1)
-        return jnp.where(ahead, jnp.where(col < SLOT, col, -1), last)
+    def beside_lane(layer, col):
+        last = jnp.where(col >= 128 - SLOT, 32 * layer + col - 128 + 2 * SLOT, -1)
+        return jnp.where(ahead, jnp.where(col < SLOT, 32 * layer + col, -1), last)
 
     def write_beside(number, total):
-        for k in range(4):
-            dense[number, k, 8:48, :] = total[40 * k : 40 * k + 40] + edge_dense[number, k, 8:48, :]
-
-    spread_wells(info, base, beside_lane, write_beside)
+        for t in range(1, 6):
+            rows = slice(8 * t, 8 * t + 8)
+            for k in range(4):
+                value = total[8 * t - 8 : 8 * t]
+                value = pltpu.roll(value, 128 - 32 * k, 1) if k else value
+                dense[number, k, rows, :] = jnp.where(beside, value, edge_dense[number, k, rows, :])
+
+    spread_wells(info, base, lambda layer: 0, 48, beside_lane, write_beside)
 
     def emit(group):
         def write(k, t, value):
@@ -587,14 +594,14 @@
         name="pack_own",
     )(own)
     strip = shape(2 * PACKED + 2, 8, 128)
-    far, near = pl.pallas_call(
+    near, far = pl.pallas_call(
         pack_cols,
         out_shape=(strip, strip),
         compiler_params=limit,
         name="pack_cols",
     )(own, own_far, own_near, row_far, row_near)
+    col_near = swapped(near, "gy", 0)
     col_far = swapped(far, "gy", 1)
-    col_near = swapped(near, "gy", 0)
     scratch = [pltpu.VMEM((COUNT, ROWS, 128), f32), pltpu.VMEM((7, 4, ROWS, 128), f32)]
     scratch += [pltpu.VMEM((4, ROWS, 128), jnp.int32)]
     scratch += [pltpu.VMEM((count, ROWS, 128), f32) for count in SCRATCH]
@@ -613,7 +620,7 @@
         scratch_shapes=[pltpu.VMEM((11, 8, 128), f32)] * 2 + [pltpu.SemaphoreType.DMA((6,))] + scratch,
         compiler_params=limit,
         name="model_edge",
-    )(col_far, col_near, edge, edge_dense, center)
+    )(col_near, col_far, edge, edge_dense, center)
 
 
 def solution(mesh):

time: 18.2 us -> 19 us (1.044)
  the two profiles are of different devices: /device:TPU:0 before, /device:TPU:20 now
where the time goes in v1:
time: 19 us; the launch traced here: 18.8 us
  starting transfers between devices  7.6 us (40%)
  waiting for transfers between devices  5.29 us (28%)
  Pallas kernels  5.27 us (28%)
  between operations  0.67 us (4%)
    ppermute x4, starting transfers between devices, swapped(): return lax.ppermute(value, axis, pairs)  7.6 us
    ppermute x4, waiting for transfers between devices, swapped(): return lax.ppermute(value, axis, pairs)  5.29 us
    pallas_call x1, Pallas kernels, on_device(): pl.pallas_call(model_edge, out_shape=(shape(*tx.shape), shape(*ty.shape),...  2.4 us
    pallas_call x1, Pallas kernels, on_device(): pl.pallas_call(model_center, out_shape=(shape(11, 16, 128), shape(COUNT,...  1.49 us
    pallas_call x1, Pallas kernels, on_device(): pl.pallas_call(pack_rows, out_shape=(shape(COUNT + 1, 16, 128), strip, st...  0.99 us
  transfers between devices with their start and end apart: 4, of which 2 were waited for; matrix products, arithmetic and copies ran while one was open for 0% of the time, Pallas kernels for 9%

profile of v1, /device:TPU:20, one launch (start us, length us, event | category | flops | bytes accessed | tf_op | source)
XLA Modules:
  0.0 18.8 jit_solution(16718744104429959263)
XLA Ops:
  0.6 1.0 %pack_rows.1 = (f32[28,16,128]{2,1,0:T(8,128)S(1)}, f32[31,8,128]{2,1,0:T(8,128)S(1)}, f32[31,8,128]{2,1,0:T(8,128)S(1)}) custom-call(f32[4,16,128]{2,1,0:T(8,128)} %refs_0_.1, f32[4,16,128]{2,1,0:T(8,128)} %refs_1_.1, f32[4,16,128]{2,1,0:T(8,128)} %refs_2_.1, f32[4,16,128]{2,1,0:T(8,128)} %refs_3_.1, f32[3,16,128]{2,1,0:T(8,128)} %refs_4_.1, ...), custom_call_target="tpu_custom_call" | custom-call | tf_op jit(solution)/shard_map/pack_rows/pallas_call | solution.py:576
  1.6 1.9 %collective-permute-start = (f32[31,8,128]{2,1,0:T(8,128)S(1)}, f32[31,8,128]{2,1,0:T(8,128)S(1)}, u32[]{:S(2)}, u32[]{:S(2)}) collective-permute-start(f32[31,8,128]{2,1,0:T(8,128)S(1)} %get-tuple-element.16), channel_id=1, source_target_pairs={{4,8},{8,4},{12,16},{16,12},{20,24},{24,20},{5,9},{9,5},{13,17},{1... | collective-permute-start | bytes 380936 | tf_op jit(solution)/shard_map/ppermute | solution.py:563
  3.6 1.7 %collective-permute-start.1 = (f32[31,8,128]{2,1,0:T(8,128)S(1)}, f32[31,8,128]{2,1,0:T(8,128)S(1)}, u32[]{:S(2)}, u32[]{:S(2)}) collective-permute-start(f32[31,8,128]{2,1,0:T(8,128)S(1)} %get-tuple-element.17), channel_id=1, source_target_pairs={{0,4},{4,0},{8,12},{12,8},{16,20},{20,16},{24,28},{28,24},{1,5},{5... | collective-permute-start | bytes 380936 | tf_op jit(solution)/shard_map/ppermute | solution.py:563
  5.3 0.2 %pack_own.1 = (f32[4,8,128]{2,1,0:T(8,128)S(1)}, f32[4,8,128]{2,1,0:T(8,128)S(1)}) custom-call(f32[28,16,128]{2,1,0:T(8,128)S(1)} %get-tuple-element.13.own), custom_call_target="tpu_custom_call" | custom-call | flops 99999997952 | bytes 268435456 | tf_op jit(solution)/shard_map/pack_own/pallas_call | solution.py:589
  5.5 2.4 %collective-permute-done.row_far = f32[31,8,128]{2,1,0:T(8,128)S(1)} collective-permute-done((f32[31,8,128]{2,1,0:T(8,128)S(1)}, f32[31,8,128]{2,1,0:T(8,128)S(1)}, u32[]{:S(2)}, u32[]{:S(2)}) %collective-permute-start) | collective-permute-done | bytes 127008 | tf_op jit(solution)/shard_map/ppermute | solution.py:563
  7.9 0.0 collective-permute-done.1.row_near
  7.9 0.2 %pack_cols.1 = (f32[10,8,128]{2,1,0:T(8,128)S(1)}, f32[10,8,128]{2,1,0:T(8,128)S(1)}) custom-call(f32[28,16,128]{2,1,0:T(8,128)S(1)} %get-tuple-element.13.own, f32[4,8,128]{2,1,0:T(8,128)S(1)} %get-tuple-element.14.own_far, f32[4,8,128]{2,1,0:T(8,128)S(1)} %get-tuple-element.15.own_near, f32[31,8,128]{2,1,0:T(8,128)S(1)} %collective-permute-done.row_far, ...), custom_call_target="tpu_custom_call" | custom-call | tf_op jit(solution)/shard_map/pack_cols/pallas_call | solution.py:597
  8.1 1.6 %collective-permute-start.2 = (f32[10,8,128]{2,1,0:T(8,128)S(1)}, f32[10,8,128]{2,1,0:T(8,128)S(1)}, u32[]{:S(2)}, u32[]{:S(2)}) collective-permute-start(f32[10,8,128]{2,1,0:T(8,128)S(1)} %get-tuple-element.18), channel_id=1, source_target_pairs={{0,1},{1,0},{2,3},{3,2},{4,5},{5,4},{6,7},{7,6},{8,9},{9,8},{10,11... | collective-permute-start | bytes 122888 | tf_op jit(solution)/shard_map/ppermute | solution.py:563
  9.6 2.4 %collective-permute-start.3 = (f32[10,8,128]{2,1,0:T(8,128)S(1)}, f32[10,8,128]{2,1,0:T(8,128)S(1)}, u32[]{:S(2)}, u32[]{:S(2)}) collective-permute-start(f32[10,8,128]{2,1,0:T(8,128)S(1)} %get-tuple-element.19), channel_id=1, source_target_pairs={{1,2},{2,1},{5,6},{6,5},{9,10},{10,9},{13,14},{14,13},{17,18},{18,... | collective-permute-start | bytes 122888 | tf_op jit(solution)/shard_map/ppermute | solution.py:563
  12.0 1.5 %model_center.1 = (f32[11,16,128]{2,1,0:T(8,128)S(1)}, f32[27,56,128]{2,1,0:T(8,128)S(1)}, f32[7,4,56,128]{3,2,1,0:T(8,128)S(1)}) custom-call(f32[28,16,128]{2,1,0:T(8,128)S(1)} %get-tuple-element.13.own, f32[31,8,128]{2,1,0:T(8,128)S(1)} %collective-permute-done.row_far, f32[31,8,128]{2,1,0:T(8,128)S(1)} %collective-permute-done.1.row_near), custom_call_target="tpu_custom_call" | custom-call | flops 99999997952 | bytes 268435456 | tf_op jit(solution)/shard_map/model_center/pallas_call | solution.py:608
  13.5 0.0 collective-permute-done.2.col_near
  13.5 2.9 %collective-permute-done.3.col_far = f32[10,8,128]{2,1,0:T(8,128)S(1)} collective-permute-done((f32[10,8,128]{2,1,0:T(8,128)S(1)}, f32[10,8,128]{2,1,0:T(8,128)S(1)}, u32[]{:S(2)}, u32[]{:S(2)}) %collective-permute-start.3) | collective-permute-done | bytes 40992 | tf_op jit(solution)/shard_map/ppermute | solution.py:563
  16.4 2.4 %model_edge.1 = (f32[4,16,128]{2,1,0:T(8,128)}, f32[4,16,128]{2,1,0:T(8,128)}, f32[3,16,128]{2,1,0:T(8,128)}) custom-call(f32[10,8,128]{2,1,0:T(8,128)S(1)} %collective-permute-done.2.col_near, f32[10,8,128]{2,1,0:T(8,128)S(1)} %collective-permute-done.3.col_far, f32[27,56,128]{2,1,0:T(8,128)S(1)} %get-tuple-element.20.edge, ...), custom_call_target="tpu_custom_call" | custom-call | tf_op jit(solution)/shard_map/model_edge/pallas_call | solution.py:616
Async XLA Ops:
  1.6 6.2 %collective-permute-start = (f32[31,8,128]{2,1,0:T(8,128)S(1)}, f32[31,8,128]{2,1,0:T(8,128)S(1)}, u32[]{:S(2)}, u32[]{:S(2)}) collective-permute-start(f32[31,8,128]{2,1,0:T(8,128)S(1)} %get-tuple-element.16), channel_id=1, source_target_pairs={{4,8},{8,4},{12,16},{16,12},{20,24},{24,20},{5,9},{9,5},{13,17},{1... | collective-permute-start | bytes 380936 | tf_op jit(solution)/shard_map/ppermute | solution.py:563
  3.6 4.3 %collective-permute-start.1 = (f32[31,8,128]{2,1,0:T(8,128)S(1)}, f32[31,8,128]{2,1,0:T(8,128)S(1)}, u32[]{:S(2)}, u32[]{:S(2)}) collective-permute-start(f32[31,8,128]{2,1,0:T(8,128)S(1)} %get-tuple-element.17), channel_id=1, source_target_pairs={{0,4},{4,0},{8,12},{12,8},{16,20},{20,16},{24,28},{28,24},{1,5},{5... | collective-permute-start | bytes 380936 | tf_op jit(solution)/shard_map/ppermute | solution.py:563
  8.1 5.4 %collective-permute-start.2 = (f32[10,8,128]{2,1,0:T(8,128)S(1)}, f32[10,8,128]{2,1,0:T(8,128)S(1)}, u32[]{:S(2)}, u32[]{:S(2)}) collective-permute-start(f32[10,8,128]{2,1,0:T(8,128)S(1)} %get-tuple-element.18), channel_id=1, source_target_pairs={{0,1},{1,0},{2,3},{3,2},{4,5},{5,4},{6,7},{7,6},{8,9},{9,8},{10,11... | collective-permute-start | bytes 122888 | tf_op jit(solution)/shard_map/ppermute | solution.py:563
  9.6 6.8 %collective-permute-start.3 = (f32[10,8,128]{2,1,0:T(8,128)S(1)}, f32[10,8,128]{2,1,0:T(8,128)S(1)}, u32[]{:S(2)}, u32[]{:S(2)}) collective-permute-start(f32[10,8,128]{2,1,0:T(8,128)S(1)} %get-tuple-element.19), channel_id=1, source_target_pairs={{1,2},{2,1},{5,6},{6,5},{9,10},{10,9},{13,14},{14,13},{17,18},{18,... | collective-permute-start | bytes 122888 | tf_op jit(solution)/shard_map/ppermute | solution.py:563

commit v2 on v1

--- a/solution.py
+++ b/solution.py
@@ -129,7 +129,7 @@
         pack_pairs(lambda g: own[g, rows, :], far, near, 2 * tile)
 
 
-def pack_cols(own, own_far, own_near, row_far, row_near, near, far):
+def pack_cols(own, own_far, own_near, row_far, row_near, far, near):
     low, high = sorted_ends("gx", row_far, row_near)
     for out, part in ((far, own_far), (near, own_near)):
         for at in range(PACKED):
@@ -192,11 +192,11 @@
     return lax.shift_right_logical(lax.broadcasted_iota(jnp.int32, (1, info.shape[1]), 1), 6)
 
 
-SCRATCH = (4,) * 11 + (11,) * 4 + (4,) * 9
+SCRATCH = (4,) * 12 + (11,) * 4 + (4,) * 9
 
 
 def simulate(fld, dense, upi, scratch, emit_x, emit_y, emit_z, tile_done=None):
-    (rcp, tym, q0, p1, q1, p2, f0, d0, s1, f1, d1, fup0, fup1, dp1, dp2,
+    (rcp, tym, per, q0, p1, q1, p2, f0, d0, s1, f1, d1, fup0, fup1, dp1, dp2,
      sig2, psi2, psi1, mup2, muq1, mup1, muq0, flux, rest) = scratch
     PB, SB, XB, YB, ZB, VB = (GROUPS[name][0] for name in ORDER[:6])
 
@@ -229,6 +229,7 @@
             volume = here(fld, VB + k, t)
             volume = jnp.where(volume == 0.0, 1.0, volume)
             put(fld, VB + k, t, volume)
+            put(per, k, t, time_step * pl.reciprocal(volume))
             west = left(here(fld, YB + k, t))
             put(tym, k, t, west)
             total = volume + (here(fld, XB + k, t) + above(fld, XB + k, t)) + (here(fld, YB + k, t) + west)
@@ -236,7 +237,7 @@
                 total = total + here(fld, ZB + k, t)
             if k > 0:
                 total = total + here(fld, ZB + k - 1, t)
-            put(rcp, k, t, 1.0 / total)
+            put(rcp, k, t, pl.reciprocal(total))
 
     def neighbours(ref, base, k, t):
         value = here(ref, base + k, t)
@@ -257,7 +258,7 @@
     def put_mobility(value, k, t, mobile, slope):
         rest_of = 1.0 - value
         wetted = value * value
-        inverse = 1.0 / (wetted + 0.5 * rest_of * rest_of)
+        inverse = pl.reciprocal(wetted + 0.5 * rest_of * rest_of)
         put(mobile, k, t, wetted * inverse)
         put(slope, k, t, value * rest_of * (inverse * inverse))
 
@@ -291,7 +292,7 @@
                     put(dp, 8 + k, t, drop_z)
                     below = here(fld, ZB + k, t) * up_z * drop_z
                     net = net + below
-                finish(here(sat, sat_base + k, t) - time_step * net / here(fld, VB + k, t), k, t)
+                finish(here(sat, sat_base + k, t) - net * here(per, k, t), k, t)
 
     tiles = range(1, 5)
     relax(q0, fld, PB, fld, PB, SRC0, range(1, 6))
@@ -311,7 +312,7 @@
     def finish_second(moved, k, t):
         miss = here(dense.at[CNT], k, t) * moved - here(dense.at[OS1], k, t)
         put(sig2, k, t, miss)
-        put(psi2, k, t, time_step * miss / here(fld, VB + k, t))
+        put(psi2, k, t, miss * here(per, k, t))
 
     transport(p2, s1, 0, f1, 1, fup1, dp2, finish_second)
 
@@ -347,7 +348,7 @@
             put(mup2, k, t, press * here(rcp, k, t))
             sigma = here(sig2, k, t) + satur * here(d1, k, t)
             sigma = sigma + (count * here(s1, k, t) - here(dense.at[OS0], k, t))
-            put(psi1, k, t, time_step * sigma / here(fld, VB + k, t))
+            put(psi1, k, t, sigma * here(per, k, t))
 
     for t in tiles:
         for k in range(4):
@@ -475,7 +476,7 @@
 
 
 def model_edge(
-    col_near, col_far, edge, edge_dense, center, grad_x, grad_y, grad_z, first_rows, last_rows, sems, fld, dense, upi,
+    col_far, col_near, edge, edge_dense, center, grad_x, grad_y, grad_z, first_rows, last_rows, sems, fld, dense, upi,
     *scratch
 ):
     before, after = sorted_ends("gy", col_far, col_near)
@@ -594,14 +595,14 @@
         name="pack_own",
     )(own)
     strip = shape(2 * PACKED + 2, 8, 128)
-    near, far = pl.pallas_call(
+    far, near = pl.pallas_call(
         pack_cols,
         out_shape=(strip, strip),
         compiler_params=limit,
         name="pack_cols",
     )(own, own_far, own_near, row_far, row_near)
+    col_far = swapped(far, "gy", 1)
     col_near = swapped(near, "gy", 0)
-    col_far = swapped(far, "gy", 1)
     scratch = [pltpu.VMEM((COUNT, ROWS, 128), f32), pltpu.VMEM((7, 4, ROWS, 128), f32)]
     scratch += [pltpu.VMEM((4, ROWS, 128), jnp.int32)]
     scratch += [pltpu.VMEM((count, ROWS, 128), f32) for count in SCRATCH]
@@ -620,7 +621,7 @@
         scratch_shapes=[pltpu.VMEM((11, 8, 128), f32)] * 2 + [pltpu.SemaphoreType.DMA((6,))] + scratch,
         compiler_params=limit,
         name="model_edge",
-    )(col_near, col_far, edge, edge_dense, center)
+    )(col_far, col_near, edge, edge_dense, center)
 
 
 def solution(mesh):

time: 19 us -> 18.2 us (0.958)
  the two profiles are of different devices: /device:TPU:20 before, /device:TPU:0 now
where the time goes in v2:
time: 18.2 us; the launch traced here: 18 us
  starting transfers between devices  10.1 us (55%)
  Pallas kernels  5.27 us (29%)
  waiting for transfers between devices  1.98 us (11%)
  between operations  0.68 us (4%)
    ppermute x4, starting transfers between devices, swapped(): return lax.ppermute(value, axis, pairs)  10.1 us
    pallas_call x1, Pallas kernels, on_device(): pl.pallas_call(model_edge, out_shape=(shape(*tx.shape), shape(*ty.shape),...  2.41 us
    ppermute x4, waiting for transfers between devices, swapped(): return lax.ppermute(value, axis, pairs)  1.98 us
    pallas_call x1, Pallas kernels, on_device(): pl.pallas_call(model_center, out_shape=(shape(11, 16, 128), shape(COUNT,...  1.48 us
    pallas_call x1, Pallas kernels, on_device(): pl.pallas_call(pack_rows, out_shape=(shape(COUNT + 1, 16, 128), strip, st...  0.99 us
  transfers between devices with their start and end apart: 4, of which 2 were waited for; matrix products, arithmetic and copies ran while one was open for 0% of the time, Pallas kernels for 9%

profile of v2, /device:TPU:0, one launch (start us, length us, event | category | flops | bytes accessed | tf_op | source)
XLA Modules:
  0.0 18.0 jit_solution(9437970191353968644)
XLA Ops:
  0.6 1.0 %pack_rows.1 = (f32[28,16,128]{2,1,0:T(8,128)S(1)}, f32[31,8,128]{2,1,0:T(8,128)S(1)}, f32[31,8,128]{2,1,0:T(8,128)S(1)}) custom-call(f32[4,16,128]{2,1,0:T(8,128)} %refs_0_.1, f32[4,16,128]{2,1,0:T(8,128)} %refs_1_.1, f32[4,16,128]{2,1,0:T(8,128)} %refs_2_.1, f32[4,16,128]{2,1,0:T(8,128)} %refs_3_.1, f32[3,16,128]{2,1,0:T(8,128)} %refs_4_.1, ...), custom_call_target="tpu_custom_call" | custom-call | tf_op jit(solution)/shard_map/pack_rows/pallas_call | solution.py:577
  1.6 0.7 %collective-permute-start = (f32[31,8,128]{2,1,0:T(8,128)S(1)}, f32[31,8,128]{2,1,0:T(8,128)S(1)}, u32[]{:S(2)}, u32[]{:S(2)}) collective-permute-start(f32[31,8,128]{2,1,0:T(8,128)S(1)} %get-tuple-element.16), channel_id=1, source_target_pairs={{4,8},{8,4},{12,16},{16,12},{20,24},{24,20},{5,9},{9,5},{13,17},{1... | collective-permute-start | bytes 380936 | tf_op jit(solution)/shard_map/ppermute | solution.py:564
  2.3 4.4 %collective-permute-start.1 = (f32[31,8,128]{2,1,0:T(8,128)S(1)}, f32[31,8,128]{2,1,0:T(8,128)S(1)}, u32[]{:S(2)}, u32[]{:S(2)}) collective-permute-start(f32[31,8,128]{2,1,0:T(8,128)S(1)} %get-tuple-element.17), channel_id=1, source_target_pairs={{0,4},{4,0},{8,12},{12,8},{16,20},{20,16},{24,28},{28,24},{1,5},{5... | collective-permute-start | bytes 380936 | tf_op jit(solution)/shard_map/ppermute | solution.py:564
  6.8 0.2 %pack_own.1 = (f32[4,8,128]{2,1,0:T(8,128)S(1)}, f32[4,8,128]{2,1,0:T(8,128)S(1)}) custom-call(f32[28,16,128]{2,1,0:T(8,128)S(1)} %get-tuple-element.13.own), custom_call_target="tpu_custom_call" | custom-call | flops 99999997952 | bytes 268435456 | tf_op jit(solution)/shard_map/pack_own/pallas_call | solution.py:590
  6.9 0.0 collective-permute-done.row_far
  7.0 0.8 %collective-permute-done.1.row_near = f32[31,8,128]{2,1,0:T(8,128)S(1)} collective-permute-done((f32[31,8,128]{2,1,0:T(8,128)S(1)}, f32[31,8,128]{2,1,0:T(8,128)S(1)}, u32[]{:S(2)}, u32[]{:S(2)}) %collective-permute-start.1) | collective-permute-done | bytes 127008 | tf_op jit(solution)/shard_map/ppermute | solution.py:564
  7.7 0.2 %pack_cols.1 = (f32[10,8,128]{2,1,0:T(8,128)S(1)}, f32[10,8,128]{2,1,0:T(8,128)S(1)}) custom-call(f32[28,16,128]{2,1,0:T(8,128)S(1)} %get-tuple-element.13.own, f32[4,8,128]{2,1,0:T(8,128)S(1)} %get-tuple-element.14.own_far, f32[4,8,128]{2,1,0:T(8,128)S(1)} %get-tuple-element.15.own_near, f32[31,8,128]{2,1,0:T(8,128)S(1)} %collective-permute-done.row_far, ...), custom_call_target="tpu_custom_call" | custom-call | tf_op jit(solution)/shard_map/pack_cols/pallas_call | solution.py:598
  7.9 0.7 %collective-permute-start.2 = (f32[10,8,128]{2,1,0:T(8,128)S(1)}, f32[10,8,128]{2,1,0:T(8,128)S(1)}, u32[]{:S(2)}, u32[]{:S(2)}) collective-permute-start(f32[10,8,128]{2,1,0:T(8,128)S(1)} %get-tuple-element.18), channel_id=1, source_target_pairs={{1,2},{2,1},{5,6},{6,5},{9,10},{10,9},{13,14},{14,13},{17,18},{18,... | collective-permute-start | bytes 122888 | tf_op jit(solution)/shard_map/ppermute | solution.py:564
  8.6 4.3 %collective-permute-start.3 = (f32[10,8,128]{2,1,0:T(8,128)S(1)}, f32[10,8,128]{2,1,0:T(8,128)S(1)}, u32[]{:S(2)}, u32[]{:S(2)}) collective-permute-start(f32[10,8,128]{2,1,0:T(8,128)S(1)} %get-tuple-element.19), channel_id=1, source_target_pairs={{0,1},{1,0},{2,3},{3,2},{4,5},{5,4},{6,7},{7,6},{8,9},{9,8},{10,11... | collective-permute-start | bytes 122888 | tf_op jit(solution)/shard_map/ppermute | solution.py:564
  12.9 1.5 %model_center.1 = (f32[11,16,128]{2,1,0:T(8,128)S(1)}, f32[27,56,128]{2,1,0:T(8,128)S(1)}, f32[7,4,56,128]{3,2,1,0:T(8,128)S(1)}) custom-call(f32[28,16,128]{2,1,0:T(8,128)S(1)} %get-tuple-element.13.own, f32[31,8,128]{2,1,0:T(8,128)S(1)} %collective-permute-done.row_far, f32[31,8,128]{2,1,0:T(8,128)S(1)} %collective-permute-done.1.row_near), custom_call_target="tpu_custom_call" | custom-call | flops 99999997952 | bytes 268435456 | tf_op jit(solution)/shard_map/model_center/pallas_call | solution.py:609
  14.4 0.0 collective-permute-done.2.col_far
  14.4 1.2 %collective-permute-done.3.col_near = f32[10,8,128]{2,1,0:T(8,128)S(1)} collective-permute-done((f32[10,8,128]{2,1,0:T(8,128)S(1)}, f32[10,8,128]{2,1,0:T(8,128)S(1)}, u32[]{:S(2)}, u32[]{:S(2)}) %collective-permute-start.3) | collective-permute-done | bytes 40992 | tf_op jit(solution)/shard_map/ppermute | solution.py:564
  15.6 2.4 %model_edge.1 = (f32[4,16,128]{2,1,0:T(8,128)}, f32[4,16,128]{2,1,0:T(8,128)}, f32[3,16,128]{2,1,0:T(8,128)}) custom-call(f32[10,8,128]{2,1,0:T(8,128)S(1)} %collective-permute-done.2.col_far, f32[10,8,128]{2,1,0:T(8,128)S(1)} %collective-permute-done.3.col_near, f32[27,56,128]{2,1,0:T(8,128)S(1)} %get-tuple-element.20.edge, ...), custom_call_target="tpu_custom_call" | custom-call | tf_op jit(solution)/shard_map/model_edge/pallas_call | solution.py:617
Async XLA Ops:
  1.6 5.3 %collective-permute-start = (f32[31,8,128]{2,1,0:T(8,128)S(1)}, f32[31,8,128]{2,1,0:T(8,128)S(1)}, u32[]{:S(2)}, u32[]{:S(2)}) collective-permute-start(f32[31,8,128]{2,1,0:T(8,128)S(1)} %get-tuple-element.16), channel_id=1, source_target_pairs={{4,8},{8,4},{12,16},{16,12},{20,24},{24,20},{5,9},{9,5},{13,17},{1... | collective-permute-start | bytes 380936 | tf_op jit(solution)/shard_map/ppermute | solution.py:564
  2.3 5.4 %collective-permute-start.1 = (f32[31,8,128]{2,1,0:T(8,128)S(1)}, f32[31,8,128]{2,1,0:T(8,128)S(1)}, u32[]{:S(2)}, u32[]{:S(2)}) collective-permute-start(f32[31,8,128]{2,1,0:T(8,128)S(1)} %get-tuple-element.17), channel_id=1, source_target_pairs={{0,4},{4,0},{8,12},{12,8},{16,20},{20,16},{24,28},{28,24},{1,5},{5... | collective-permute-start | bytes 380936 | tf_op jit(solution)/shard_map/ppermute | solution.py:564
  7.9 6.5 %collective-permute-start.2 = (f32[10,8,128]{2,1,0:T(8,128)S(1)}, f32[10,8,128]{2,1,0:T(8,128)S(1)}, u32[]{:S(2)}, u32[]{:S(2)}) collective-permute-start(f32[10,8,128]{2,1,0:T(8,128)S(1)} %get-tuple-element.18), channel_id=1, source_target_pairs={{1,2},{2,1},{5,6},{6,5},{9,10},{10,9},{13,14},{14,13},{17,18},{18,... | collective-permute-start | bytes 122888 | tf_op jit(solution)/shard_map/ppermute | solution.py:564
  8.6 7.0 %collective-permute-start.3 = (f32[10,8,128]{2,1,0:T(8,128)S(1)}, f32[10,8,128]{2,1,0:T(8,128)S(1)}, u32[]{:S(2)}, u32[]{:S(2)}) collective-permute-start(f32[10,8,128]{2,1,0:T(8,128)S(1)} %get-tuple-element.19), channel_id=1, source_target_pairs={{0,1},{1,0},{2,3},{3,2},{4,5},{5,4},{6,7},{7,6},{8,9},{9,8},{10,11... | collective-permute-start | bytes 122888 | tf_op jit(solution)/shard_map/ppermute | solution.py:564

commit v3 on v2

--- a/solution.py
+++ b/solution.py
@@ -192,12 +192,13 @@
     return lax.shift_right_logical(lax.broadcasted_iota(jnp.int32, (1, info.shape[1]), 1), 6)
 
 
-SCRATCH = (4,) * 12 + (11,) * 4 + (4,) * 9
+SCRATCH = (4,) * 12 + (11,) * 4 + (4,) * 13
 
 
 def simulate(fld, dense, upi, scratch, emit_x, emit_y, emit_z, tile_done=None):
     (rcp, tym, per, q0, p1, q1, p2, f0, d0, s1, f1, d1, fup0, fup1, dp1, dp2,
-     sig2, psi2, psi1, mup2, muq1, mup1, muq0, flux, rest) = scratch
+     sig2, psi2, psi1, mup2, muq1, mup1, muq0, flux, rest,
+     west0, west1, drop1, drop2, upl) = scratch
     PB, SB, XB, YB, ZB, VB = (GROUPS[name][0] for name in ORDER[:6])
 
     def here(ref, k, t):
@@ -232,6 +233,7 @@
             put(per, k, t, time_step * pl.reciprocal(volume))
             west = left(here(fld, YB + k, t))
             put(tym, k, t, west)
+            put(upl, k, t, left(here(upi, k, t)))
             total = volume + (here(fld, XB + k, t) + above(fld, XB + k, t)) + (here(fld, YB + k, t) + west)
             if k < 3:
                 total = total + here(fld, ZB + k, t)
@@ -265,7 +267,10 @@
     def bit(k, t, number):
         return (here(upi, k, t) & (1 << number)) != 0
 
-    def transport(pressure, sat, sat_base, mobile, n, fup, dp, finish):
+    def bit_left(k, t, number):
+        return (here(upl, k, t) & (1 << number)) != 0
+
+    def transport(pressure, sat, sat_base, mobile, n, fup, dp, wests, drops, finish):
         for t in range(1, 5):
             below = None
             for k in range(4):
@@ -282,7 +287,11 @@
                 flux_x = here(fld, XB + k, t) * up_x * drop_x
                 flux_y = here(fld, YB + k, t) * up_y * drop_y
                 put(flux, k, t, flux_x)
-                net = (flux_x - above(flux, k, t)) + (flux_y - left(flux_y))
+                west = jnp.where(bit_left(k, t, 3 * n + 1), left(mob), mob)
+                drop_w = left(pres) - pres
+                put(wests, k, t, west)
+                put(drops, k, t, drop_w)
+                net = (flux_x - above(flux, k, t)) + (flux_y - here(tym, k, t) * west * drop_w)
                 if k > 0:
                     net = net - below
                 if k < 3:
@@ -305,7 +314,7 @@
         put(s1, k, t, moved)
         put_mobility(moved, k, t, f1, d1)
 
-    transport(p1, fld, SB, f0, 0, fup0, dp1, finish_first)
+    transport(p1, fld, SB, f0, 0, fup0, dp1, west0, drop1, finish_first)
     relax(q1, p1, 0, p1, 0, SRC1, tiles)
     relax(p2, q1, 0, p1, 0, SRC1, tiles)
 
@@ -314,7 +323,7 @@
         put(sig2, k, t, miss)
         put(psi2, k, t, miss * here(per, k, t))
 
-    transport(p2, s1, 0, f1, 1, fup1, dp2, finish_second)
+    transport(p2, s1, 0, f1, 1, fup1, dp2, west1, drop2, finish_second)
 
     for t in tiles:
         below_h = below_r = None
@@ -330,8 +339,10 @@
             s_y = jnp.where(bit(k, t, 4), k_y, 0.0)
             put(flux, k, t, h_x)
             put(rest, k, t, k_x - s_x)
-            press = (h_x - above(flux, k, t)) + (h_y - left(h_y))
-            satur = (s_x + above(rest, k, t)) + (s_y + left(k_y - s_y))
+            phi_w = (psi - left(psi)) * here(tym, k, t)
+            r_w = jnp.where(bit_left(k, t, 4), 0.0, phi_w * here(drop2, k, t))
+            press = (h_x - above(flux, k, t)) + (h_y - phi_w * here(west1, k, t))
+            satur = (s_x + above(rest, k, t)) + (s_y + r_w)
             if k > 0:
                 press = press - below_h
                 satur = satur + below_r
@@ -361,7 +372,8 @@
             h_x = (down(psi1, k, t) - psi) * here(fld, XB + k, t) * here(fup0, k, t)
             h_y = (right(psi) - psi) * here(fld, YB + k, t) * here(fup0, 4 + k, t)
             put(flux, k, t, h_x)
-            press = (h_x - above(flux, k, t)) + (h_y - left(h_y))
+            h_w = (psi - left(psi)) * here(tym, k, t) * here(west0, k, t)
+            press = (h_x - above(flux, k, t)) + (h_y - h_w)
             if k > 0:
                 press = press - below_h
             if k < 3:
@@ -606,6 +618,7 @@
     scratch = [pltpu.VMEM((COUNT, ROWS, 128), f32), pltpu.VMEM((7, 4, ROWS, 128), f32)]
     scratch += [pltpu.VMEM((4, ROWS, 128), jnp.int32)]
     scratch += [pltpu.VMEM((count, ROWS, 128), f32) for count in SCRATCH]
+    scratch += [pltpu.VMEM((4, ROWS, 128), jnp.int32)]
     center, edge, edge_dense = pl.pallas_call(
         model_center,
         out_shape=(shape(11, 16, 128), shape(COUNT, ROWS, 128), shape(7, 4, ROWS, 128)),

time: 18.2 us -> 18.1 us (level)
  no operation moved by 1% of the time
where the time goes in v3:
time: 18.1 us; the launch traced here: 17.9 us
  starting transfers between devices  10.1 us (56%)
  Pallas kernels  5.12 us (28%)
  waiting for transfers between devices  2.06 us (11%)
  between operations  0.68 us (4%)
    ppermute x4, starting transfers between devices, swapped(): return lax.ppermute(value, axis, pairs)  10.1 us
    pallas_call x1, Pallas kernels, on_device(): pl.pallas_call(model_edge, out_shape=(shape(*tx.shape), shape(*ty.shape),...  2.34 us
    ppermute x4, waiting for transfers between devices, swapped(): return lax.ppermute(value, axis, pairs)  2.06 us
    pallas_call x1, Pallas kernels, on_device(): pl.pallas_call(model_center, out_shape=(shape(11, 16, 128), shape(COUNT,...  1.4 us
    pallas_call x1, Pallas kernels, on_device(): pl.pallas_call(pack_rows, out_shape=(shape(COUNT + 1, 16, 128), strip, st...  0.99 us
  transfers between devices with their start and end apart: 4, of which 2 were waited for; matrix products, arithmetic and copies ran while one was open for 0% of the time, Pallas kernels for 9%

profile of v3, /device:TPU:0, one launch (start us, length us, event | category | flops | bytes accessed | tf_op | source)
XLA Modules:
  0.0 17.9 jit_solution(4852015945014023962)
XLA Ops:
  0.6 1.0 %pack_rows.1 = (f32[28,16,128]{2,1,0:T(8,128)S(1)}, f32[31,8,128]{2,1,0:T(8,128)S(1)}, f32[31,8,128]{2,1,0:T(8,128)S(1)}) custom-call(f32[4,16,128]{2,1,0:T(8,128)} %refs_0_.1, f32[4,16,128]{2,1,0:T(8,128)} %refs_1_.1, f32[4,16,128]{2,1,0:T(8,128)} %refs_2_.1, f32[4,16,128]{2,1,0:T(8,128)} %refs_3_.1, f32[3,16,128]{2,1,0:T(8,128)} %refs_4_.1, ...), custom_call_target="tpu_custom_call" | custom-call | tf_op jit(solution)/shard_map/pack_rows/pallas_call | solution.py:589
  1.6 0.7 %collective-permute-start = (f32[31,8,128]{2,1,0:T(8,128)S(1)}, f32[31,8,128]{2,1,0:T(8,128)S(1)}, u32[]{:S(2)}, u32[]{:S(2)}) collective-permute-start(f32[31,8,128]{2,1,0:T(8,128)S(1)} %get-tuple-element.16), channel_id=1, source_target_pairs={{4,8},{8,4},{12,16},{16,12},{20,24},{24,20},{5,9},{9,5},{13,17},{1... | collective-permute-start | bytes 380936 | tf_op jit(solution)/shard_map/ppermute | solution.py:576
  2.3 4.4 %collective-permute-start.1 = (f32[31,8,128]{2,1,0:T(8,128)S(1)}, f32[31,8,128]{2,1,0:T(8,128)S(1)}, u32[]{:S(2)}, u32[]{:S(2)}) collective-permute-start(f32[31,8,128]{2,1,0:T(8,128)S(1)} %get-tuple-element.17), channel_id=1, source_target_pairs={{0,4},{4,0},{8,12},{12,8},{16,20},{20,16},{24,28},{28,24},{1,5},{5... | collective-permute-start | bytes 380936 | tf_op jit(solution)/shard_map/ppermute | solution.py:576
  6.8 0.2 %pack_own.1 = (f32[4,8,128]{2,1,0:T(8,128)S(1)}, f32[4,8,128]{2,1,0:T(8,128)S(1)}) custom-call(f32[28,16,128]{2,1,0:T(8,128)S(1)} %get-tuple-element.13.own), custom_call_target="tpu_custom_call" | custom-call | flops 99999997952 | bytes 268435456 | tf_op jit(solution)/shard_map/pack_own/pallas_call | solution.py:602
  6.9 0.0 collective-permute-done.row_far
  7.0 0.8 %collective-permute-done.1.row_near = f32[31,8,128]{2,1,0:T(8,128)S(1)} collective-permute-done((f32[31,8,128]{2,1,0:T(8,128)S(1)}, f32[31,8,128]{2,1,0:T(8,128)S(1)}, u32[]{:S(2)}, u32[]{:S(2)}) %collective-permute-start.1) | collective-permute-done | bytes 127008 | tf_op jit(solution)/shard_map/ppermute | solution.py:576
  7.7 0.2 %pack_cols.1 = (f32[10,8,128]{2,1,0:T(8,128)S(1)}, f32[10,8,128]{2,1,0:T(8,128)S(1)}) custom-call(f32[28,16,128]{2,1,0:T(8,128)S(1)} %get-tuple-element.13.own, f32[4,8,128]{2,1,0:T(8,128)S(1)} %get-tuple-element.14.own_far, f32[4,8,128]{2,1,0:T(8,128)S(1)} %get-tuple-element.15.own_near, f32[31,8,128]{2,1,0:T(8,128)S(1)} %collective-permute-done.row_far, ...), custom_call_target="tpu_custom_call" | custom-call | tf_op jit(solution)/shard_map/pack_cols/pallas_call | solution.py:610
  7.9 0.7 %collective-permute-start.2 = (f32[10,8,128]{2,1,0:T(8,128)S(1)}, f32[10,8,128]{2,1,0:T(8,128)S(1)}, u32[]{:S(2)}, u32[]{:S(2)}) collective-permute-start(f32[10,8,128]{2,1,0:T(8,128)S(1)} %get-tuple-element.18), channel_id=1, source_target_pairs={{1,2},{2,1},{5,6},{6,5},{9,10},{10,9},{13,14},{14,13},{17,18},{18,... | collective-permute-start | bytes 122888 | tf_op jit(solution)/shard_map/ppermute | solution.py:576
  8.6 4.3 %collective-permute-start.3 = (f32[10,8,128]{2,1,0:T(8,128)S(1)}, f32[10,8,128]{2,1,0:T(8,128)S(1)}, u32[]{:S(2)}, u32[]{:S(2)}) collective-permute-start(f32[10,8,128]{2,1,0:T(8,128)S(1)} %get-tuple-element.19), channel_id=1, source_target_pairs={{0,1},{1,0},{2,3},{3,2},{4,5},{5,4},{6,7},{7,6},{8,9},{9,8},{10,11... | collective-permute-start | bytes 122888 | tf_op jit(solution)/shard_map/ppermute | solution.py:576
  12.9 1.4 %model_center.1 = (f32[11,16,128]{2,1,0:T(8,128)S(1)}, f32[27,56,128]{2,1,0:T(8,128)S(1)}, f32[7,4,56,128]{3,2,1,0:T(8,128)S(1)}) custom-call(f32[28,16,128]{2,1,0:T(8,128)S(1)} %get-tuple-element.13.own, f32[31,8,128]{2,1,0:T(8,128)S(1)} %collective-permute-done.row_far, f32[31,8,128]{2,1,0:T(8,128)S(1)} %collective-permute-done.1.row_near), custom_call_target="tpu_custom_call" | custom-call | flops 99999997952 | bytes 268435456 | tf_op jit(solution)/shard_map/model_center/pallas_call | solution.py:622
  14.3 0.0 collective-permute-done.2.col_far
  14.3 1.3 %collective-permute-done.3.col_near = f32[10,8,128]{2,1,0:T(8,128)S(1)} collective-permute-done((f32[10,8,128]{2,1,0:T(8,128)S(1)}, f32[10,8,128]{2,1,0:T(8,128)S(1)}, u32[]{:S(2)}, u32[]{:S(2)}) %collective-permute-start.3) | collective-permute-done | bytes 40992 | tf_op jit(solution)/shard_map/ppermute | solution.py:576
  15.6 2.3 %model_edge.1 = (f32[4,16,128]{2,1,0:T(8,128)}, f32[4,16,128]{2,1,0:T(8,128)}, f32[3,16,128]{2,1,0:T(8,128)}) custom-call(f32[10,8,128]{2,1,0:T(8,128)S(1)} %collective-permute-done.2.col_far, f32[10,8,128]{2,1,0:T(8,128)S(1)} %collective-permute-done.3.col_near, f32[27,56,128]{2,1,0:T(8,128)S(1)} %get-tuple-element.20.edge, ...), custom_call_target="tpu_custom_call" | custom-call | tf_op jit(solution)/shard_map/model_edge/pallas_call | solution.py:630
Async XLA Ops:
  1.6 5.3 %collective-permute-start = (f32[31,8,128]{2,1,0:T(8,128)S(1)}, f32[31,8,128]{2,1,0:T(8,128)S(1)}, u32[]{:S(2)}, u32[]{:S(2)}) collective-permute-start(f32[31,8,128]{2,1,0:T(8,128)S(1)} %get-tuple-element.16), channel_id=1, source_target_pairs={{4,8},{8,4},{12,16},{16,12},{20,24},{24,20},{5,9},{9,5},{13,17},{1... | collective-permute-start | bytes 380936 | tf_op jit(solution)/shard_map/ppermute | solution.py:576
  2.3 5.4 %collective-permute-start.1 = (f32[31,8,128]{2,1,0:T(8,128)S(1)}, f32[31,8,128]{2,1,0:T(8,128)S(1)}, u32[]{:S(2)}, u32[]{:S(2)}) collective-permute-start(f32[31,8,128]{2,1,0:T(8,128)S(1)} %get-tuple-element.17), channel_id=1, source_target_pairs={{0,4},{4,0},{8,12},{12,8},{16,20},{20,16},{24,28},{28,24},{1,5},{5... | collective-permute-start | bytes 380936 | tf_op jit(solution)/shard_map/ppermute | solution.py:576
  7.9 6.4 %collective-permute-start.2 = (f32[10,8,128]{2,1,0:T(8,128)S(1)}, f32[10,8,128]{2,1,0:T(8,128)S(1)}, u32[]{:S(2)}, u32[]{:S(2)}) collective-permute-start(f32[10,8,128]{2,1,0:T(8,128)S(1)} %get-tuple-element.18), channel_id=1, source_target_pairs={{1,2},{2,1},{5,6},{6,5},{9,10},{10,9},{13,14},{14,13},{17,18},{18,... | collective-permute-start | bytes 122888 | tf_op jit(solution)/shard_map/ppermute | solution.py:576
  8.6 7.0 %collective-permute-start.3 = (f32[10,8,128]{2,1,0:T(8,128)S(1)}, f32[10,8,128]{2,1,0:T(8,128)S(1)}, u32[]{:S(2)}, u32[]{:S(2)}) collective-permute-start(f32[10,8,128]{2,1,0:T(8,128)S(1)} %get-tuple-element.19), channel_id=1, source_target_pairs={{0,1},{1,0},{2,3},{3,2},{4,5},{5,4},{6,7},{7,6},{8,9},{9,8},{10,11... | collective-permute-start | bytes 122888 | tf_op jit(solution)/shard_map/ppermute | solution.py:576
